TPU v7x, 512 devices: a whole 4x4x16 slice. The times are simulated.
512 devices in a mesh: row: 8 (over x, z_hi), col: 8 (over y, core), dp: 8 (over z_lo).
Axes of the slice: x: 4, y: 4, z: 16 (z_hi: 2, z_lo: 8; z = z_hi * 8 + z_lo), core: 2. Of those that a mesh axis runs over, the one named last changes fastest.
Arguments:
- inputs: bfloat16 [8, 256, 4096], P('dp', 'col', 'row'), may hold values from -6 to 6
- w_gate: bfloat16 [4096, 14336], P('row', 'col'), may hold values from -0.09375 to 0.09375
- w_up: bfloat16 [4096, 14336], P('row', 'col'), may hold values from -0.09375 to 0.09375
- cotangent: bfloat16 [8, 256, 14336], P('dp', 'row', 'col'), may hold values from -6 to 6
Outputs:
- hidden: bfloat16 [8, 256, 14336], P('dp', 'row', 'col')
- grad_inputs: bfloat16 [8, 256, 4096], P('dp', 'col', 'row')
- grad_gate: bfloat16 [4096, 14336], P('row', ('col', 'dp'))
- grad_up: bfloat16 [4096, 14336], P('row', ('col', 'dp'))
All inputs are finite; a program needn't handle non-finite values.
Results may differ from a plain program's by a relative error of at most 0.028.
Values may be sent and summed in bfloat16 or wider, within the bound.
A program may use at most 64 MiB of HBM per device.

v0:
```python
import jax
import jax.numpy as jnp
from jax import lax
from jax.sharding import PartitionSpec as P


def replica_sum(everyone, own_gate, own_up):
    replicas = everyone.shape[0]
    sub_width = own_gate.shape[1]
    stacked_gate = own_gate.reshape(replicas, -1, sub_width)
    stacked_up = own_up.reshape(replicas, -1, sub_width)
    bdims = (((1,), (1,)), ((0,), (0,)))
    part_gate = lax.dot_general(everyone, stacked_gate, bdims, preferred_element_type=jnp.float32)
    part_up = lax.dot_general(everyone, stacked_up, bdims, preferred_element_type=jnp.float32)
    part_gate = lax.optimization_barrier(part_gate.astype(jnp.bfloat16))
    part_up = lax.optimization_barrier(part_up.astype(jnp.bfloat16))
    grad_gate = jnp.sum(part_gate.astype(jnp.float32), axis=0).astype(jnp.bfloat16)
    grad_up = jnp.sum(part_up.astype(jnp.float32), axis=0).astype(jnp.bfloat16)
    return (grad_gate, grad_up)


def local(inputs, w_gate, w_up, cotangent):
    ff_local = w_gate.shape[1]
    mine = lax.all_gather(inputs, "col", axis=1, tiled=True)[0]
    everyone = None
    first = jnp.dot(mine, w_gate, preferred_element_type=jnp.float32)
    second = jnp.dot(mine, w_up, preferred_element_type=jnp.float32)
    both = lax.psum_scatter(
        jnp.concatenate([first, second], axis=1).astype(jnp.bfloat16),
        "row",
        scatter_dimension=0,
        tiled=True,
    ).astype(jnp.float32)
    gate = both[:, :ff_local]
    upper = both[:, ff_local:]
    sig = jax.nn.sigmoid(gate)
    act = gate * sig
    hidden = (act * upper).astype(jnp.bfloat16)
    slope = cotangent[0].astype(jnp.float32)
    d_gate = (slope * upper * sig * (1.0 + gate * (1.0 - sig))).astype(jnp.bfloat16)
    d_up = (slope * act).astype(jnp.bfloat16)
    full_gate, full_up = (
        lax.all_gather(d_gate, "row", axis=0, tiled=True),
        lax.all_gather(d_up, "row", axis=0, tiled=True),
    )
    dims = (((1,), (1,)), ((), ()))
    term = lax.dot_general(full_gate, w_gate, dims, preferred_element_type=jnp.float32)
    grad_inputs = lax.psum_scatter(
        (term + lax.dot_general(full_up, w_up, dims, preferred_element_type=jnp.float32)).astype(
            jnp.bfloat16
        ),
        "col",
        scatter_dimension=0,
        tiled=True,
    )
    everyone = lax.all_gather(mine[None], "dp", axis=0, tiled=True)
    own_gate, own_up = (
        lax.all_to_all(full_gate, "dp", split_axis=1, concat_axis=0, tiled=True),
        lax.all_to_all(full_up, "dp", split_axis=1, concat_axis=0, tiled=True),
    )
    grad_gate, grad_up = replica_sum(everyone, own_gate, own_up)
    return (hidden[None], grad_inputs[None], grad_gate, grad_up)


def solution(mesh):
    in_specs = (P("dp", "col", "row"), P("row", "col"), P("row", "col"), P("dp", "row", "col"))
    out_specs = (
        P("dp", "row", "col"),
        P("dp", "col", "row"),
        P("row", ("col", "dp")),
        P("row", ("col", "dp")),
    )
    return jax.shard_map(local, mesh=mesh, in_specs=in_specs, out_specs=out_specs, check_vma=False)
```

profile of v0, /device:TPU:1, one launch (start us, length us, event | category | flops | bytes accessed | tf_op | source)
XLA Modules:
  0.0 509.4 jit_solution(10851406372252797893)
XLA Ops:
  8.0 0.0 copy-start
  8.0 0.0 reduce-scatter.3.cloned.1.call-start
  8.1 19.9 %all_gather.12 = bf16[1,256,512]{2,1,0:T(8,128)(2,1)S(1)} all-gather(bf16[1,32,512]{2,1,0:T(8,128)(2,1)} %param.4), channel_id=1, replica_groups=mesh['row'=8,'col'=8,'dp'=8] {'col'}, dimensions={1}, use_global_device_ids=true | all-gather | bytes 294912 | tf_op jit(solution)/shard_map/all_gather | solution.py:24
  28.0 2.2 convolution_convert_fusion
  30.2 0.6 convolution_convert_fusion.1
  30.9 1.4 pad_maximum_fusion
  32.2 0.0 reduce-scatter.3.cloned.1.call-update
  32.3 136.7 %reduce-scatter.3.cloned.1.call-done = bf16[32,3584]{1,0:T(8,128)(2,1)} async-done(((bf16[256,3584]{1,0:T(8,128)(2,1)}), bf16[32,3584]{1,0:T(8,128)(2,1)}) %reduce-scatter.3.cloned.1.call-update) | async-done | bytes 229392 | tf_op jit(solution)/shard_map/reduce_scatter | solution.py:28
  168.9 1.0 convert_element_type.38
  169.9 0.8 fusion.8
  170.7 85.7 %all_gather.13 = bf16[256,1792]{1,0:T(8,128)(2,1)S(1)} all-gather(bf16[32,1792]{1,0:T(8,128)(2,1)S(1)} %get-tuple-element.5), channel_id=1, replica_groups=mesh['row'=8,'col'=8,'dp'=8] {'row'}, dimensions={0}, use_global_device_ids=true | all-gather | bytes 1032192 | tf_op jit(solution)/shard_map/all_gather | solution.py:43
  256.4 1.3 copy.12
  257.7 4.4 all-to-all-start
  262.1 0.0 all-gather.2.cloned.1.call-start
  262.1 0.5 all-gather.2.cloned.1.call-update
  262.6 71.2 %all_gather.14 = bf16[256,1792]{1,0:T(8,128)(2,1)} all-gather(bf16[32,1792]{1,0:T(8,128)(2,1)S(1)} %get-tuple-element.4), channel_id=1, replica_groups=mesh['row'=8,'col'=8,'dp'=8] {'row'}, dimensions={0}, use_global_device_ids=true | all-gather | bytes 1032192 | tf_op jit(solution)/shard_map/all_gather | solution.py:44
  333.8 2.2 copy.13
  336.1 6.5 %all-to-all-done = bf16[256,8,224]{0,2,1:T(8,128)(2,1)} async-done(((bf16[256,8,224]{0,2,1:T(8,128)(2,1)}), bf16[256,8,224]{0,2,1:T(8,128)(2,1)}, u32[]{:S(2)}, u32[]{:S(2)}) %all-to-all-start) | async-done | bytes 917536 | tf_op jit(solution)/shard_map/all_to_all | solution.py:58
  342.6 89.9 %all-to-all-start.1 = ((bf16[256,8,224]{0,2,1:T(8,128)(2,1)}), bf16[256,8,224]{0,2,1:T(8,128)(2,1)}, u32[]{:S(2)}, u32[]{:S(2)}) async-start(bf16[256,8,224]{0,2,1:T(8,128)(2,1)} %bitcast.32), calls=%async_computation.3 | async-start | bytes 1835008 | tf_op jit(solution)/shard_map/all_to_all | solution.py:59
  432.5 0.0 reduce-scatter.5.cloned.1.call-start
  432.6 0.7 fusion.11
  433.3 0.5 copy-done.1
  433.8 0.6 copy-done.2
  434.4 1.4 fusion
  435.8 0.0 reduce-scatter.5.cloned.1.call-update
  435.8 0.0 all-gather.2.cloned.1.call-done
  435.8 3.7 convert_bitcast_fusion.1
  439.6 20.6 %all-to-all-done.1 = bf16[256,8,224]{0,2,1:T(8,128)(2,1)} async-done(((bf16[256,8,224]{0,2,1:T(8,128)(2,1)}), bf16[256,8,224]{0,2,1:T(8,128)(2,1)}, u32[]{:S(2)}, u32[]{:S(2)}) %all-to-all-start.1) | async-done | bytes 917536 | tf_op jit(solution)/shard_map/all_to_all | solution.py:59
  460.2 3.8 convert_bitcast_fusion
  463.9 2.5 reduce_sum.24
  466.4 2.5 reduce_sum.25
  469.0 33.0 %reduce-scatter.5.cloned.1.call-done = bf16[32,512]{1,0:T(8,128)(2,1)} async-done(((bf16[256,512]{1,0:T(8,128)(2,1)}), bf16[32,512]{1,0:T(8,128)(2,1)}) %reduce-scatter.5.cloned.1.call-update) | async-done | bytes 32784 | tf_op jit(solution)/shard_map/reduce_scatter | solution.py:48
  (7 shorter events, 0.0 us)
Async XLA Ops:
  8.0 22.2 %copy-start = (bf16[512,1792]{1,0:T(8,128)(2,1)S(1)}, bf16[512,1792]{1,0:T(8,128)(2,1)}, u32[]{:S(2)}) copy-start(bf16[512,1792]{1,0:T(8,128)(2,1)} %param.5) | copy-start | bytes 5505028
  8.0 160.9 %reduce-scatter.3.cloned.1.call-start = ((), (), s32[]{:S(2)}) async-start(), calls=%async_computation.4 | async-start | bytes 2064384 | tf_op jit(solution)/shard_map/reduce_scatter | solution.py:28
  28.0 2.9 copy-start.3
  32.2 137.7 %copy-start.4 = (bf16[1,32,1792]{2,1,0:T(8,128)(2,1)S(1)}, bf16[1,32,1792]{2,1,0:T(8,128)(2,1)}, u32[]{:S(2)}) copy-start(bf16[1,32,1792]{2,1,0:T(8,128)(2,1)} %param.7) | copy-start | bytes 344068
  257.7 84.9 %all-to-all-start = ((bf16[256,8,224]{0,2,1:T(8,128)(2,1)}), bf16[256,8,224]{0,2,1:T(8,128)(2,1)}, u32[]{:S(2)}, u32[]{:S(2)}) async-start(bf16[256,8,224]{0,2,1:T(8,128)(2,1)} %bitcast.33), calls=%async_computation.2 | async-start | bytes 1835008 | tf_op jit(solution)/shard_map/all_to_all | solution.py:58
  262.1 173.8 %all-gather.2.cloned.1.call-start = ((), (), s32[]{:S(2)}) async-start(), calls=%async_computation.6 | async-start | bytes 2359296 | tf_op jit(solution)/shard_map/all_gather | solution.py:56
  342.6 117.6 %all-to-all-start.1 = ((bf16[256,8,224]{0,2,1:T(8,128)(2,1)}), bf16[256,8,224]{0,2,1:T(8,128)(2,1)}, u32[]{:S(2)}, u32[]{:S(2)}) async-start(bf16[256,8,224]{0,2,1:T(8,128)(2,1)} %bitcast.32), calls=%async_computation.3 | async-start | bytes 1835008 | tf_op jit(solution)/shard_map/all_to_all | solution.py:59
  432.5 69.4 %reduce-scatter.5.cloned.1.call-start = ((), (), s32[]{:S(2)}) async-start(), calls=%async_computation.5 | async-start | bytes 294912 | tf_op jit(solution)/shard_map/reduce_scatter | solution.py:48
  432.6 1.2 copy-start.1
  432.6 1.8 copy-start.2
Sparse Core Ops, SparseCore 0:
  32.4 136.4 reduce-scatter.2
  436.8 65.1 reduce-scatter.4
Sparse Core Ops, SparseCore 1:
  264.8 137.5 all-gather.1
where the time goes:
time: 510 us; the launch traced here: 509 us
  waiting for transfers between devices  197 us (39%)
  blocking collectives  177 us (35%)
  starting transfers between devices  94.4 us (19%)
  between operations  15.6 us (3%)
  matrix products  12.5 us (2%)
  other arithmetic  8.12 us (2%)
    reduce_scatter x1, waiting for transfers between devices, local(): lax.psum_scatter(jnp.concatenate([first, second], axis=1).astype(jnp.bflo...  137 us
    all_to_all x1, starting transfers between devices, local(): lax.all_to_all(full_up, 'dp', split_axis=1, concat_axis=0, tiled=True)  89.9 us
    all_gather x1, blocking collectives, local(): lax.all_gather(d_gate, 'row', axis=0, tiled=True)  85.7 us
    all_gather x1, blocking collectives, local(): lax.all_gather(d_up, 'row', axis=0, tiled=True)  71.2 us
    reduce_scatter x1, waiting for transfers between devices, local(): lax.psum_scatter((term + lax.dot_general(full_up, w_up, dims, preferred_e...  33 us
    all_to_all x1, waiting for transfers between devices, local(): lax.all_to_all(full_up, 'dp', split_axis=1, concat_axis=0, tiled=True)  20.6 us
    all_gather x1, blocking collectives, local(): mine = lax.all_gather(inputs, 'col', axis=1, tiled=True)[0]  19.9 us
  transfers between devices with their start and end apart: 5, of which 4 were waited for; matrix products, arithmetic and copies ran while one was open for 3% of the time, Pallas kernels for 0%

commit v1 on v0

v1 whole, which is shorter than its diff:
```python
import functools

import jax
import jax.numpy as jnp
from jax import lax
from jax.experimental import pallas as pl
from jax.experimental.pallas import tpu as pltpu
from jax.sharding import PartitionSpec as P

MESH = pl.DeviceIdType.MESH
F32 = jnp.float32
BF16 = jnp.bfloat16


def wait_bytes(ref, sem):
    pltpu.make_async_copy(ref, ref, sem).wait()


def kernel(
    nx, ncol, nd, sub, pad, tb,
    in_ref, wg_ref, wu_ref, cot_ref,
    hid_ref, gi_ref, gg_ref, gu_ref,
    wg, wu, cot, wp, cotp, hidp, everyone, xsend, xrecv, zown, zsend, zrecv, dsend, dall, gsend, grecv, fsend, frecv, acc, giown,
    loc, agc_s, agc_r, agz_s, agz_r, agy_s, agy_r, x_s, x_r, z_s, z_r, dz_s, dz_r, dx_s, dx_r, g_s, g_r, f_s, f_r,
):
    row, col, d = lax.axis_index("row"), lax.axis_index("col"), lax.axis_index("dp")
    x, h = row // 2, row % 2
    nz = 2 * nd
    z = h * nd + d
    feat = wg.shape[0]

    def zdev(z2):
        return (x * 2 + z2 // nd, col, z2 % nd)

    def xdev(i):
        return (lax.rem(x + i, nx) * 2 + h, col, d)

    def cdev(i):
        return (row, lax.rem(col + i, ncol), d)

    def send(src, dst, ssem, rsem, dev):
        pltpu.make_async_remote_copy(
            src_ref=src, dst_ref=dst, send_sem=ssem, recv_sem=rsem, device_id=dev, device_id_type=MESH
        ).start()

    barrier = pltpu.get_barrier_semaphore()
    for i in range(1, ncol):
        pl.semaphore_signal(barrier, inc=1, device_id=cdev(i), device_id_type=MESH)
    for i in range(1, nx):
        pl.semaphore_signal(barrier, inc=1, device_id=xdev(i), device_id_type=MESH)
    for i in range(1, nz):
        pl.semaphore_signal(barrier, inc=1, device_id=zdev(lax.rem(z + i, nz)), device_id_type=MESH)
    loads = [
        pltpu.make_async_copy(wg_ref, wg, loc.at[0]),
        pltpu.make_async_copy(wu_ref, wu, loc.at[1]),
        pltpu.make_async_copy(cot_ref.at[0], cot, loc.at[2]),
        pltpu.make_async_copy(in_ref.at[0], everyone.at[0, pl.ds(col * tb, tb)], loc.at[3]),
    ]
    for load in loads:
        load.start()
    pl.semaphore_wait(barrier, ncol - 1 + nx - 1 + nz - 1)

    for i in range(1, ncol):
        send(in_ref.at[0], everyone.at[0, pl.ds(col * tb, tb)], agc_s, agc_r, cdev(i))
    for i in range(1, nd):
        send(in_ref.at[0], everyone.at[i, pl.ds(col * tb, tb)], agz_s, agz_r.at[i], (row, col, lax.rem(d + i, nd)))

    for load in loads:
        load.wait()

    @pl.loop(0, feat // 64)
    def _(q):
        rows = pl.ds(pl.multiple_of(q * 64, 64), 64)
        for j in range(nd):
            for k, w in enumerate((wg, wu)):
                wp[j, rows, k * pad : k * pad + sub] = w[rows, j * sub : (j + 1) * sub]
                wp[j, rows, k * pad + sub : (k + 1) * pad] = jnp.zeros((64, pad - sub), BF16)

    for j in range(nd):
        cotp[j, :, :sub] = cot[:, j * sub : (j + 1) * sub]
        cotp[j, :, sub:] = jnp.zeros((tb, pad - sub), BF16)
    acc[...] = jnp.zeros_like(acc)
    wait_bytes(everyone.at[0, pl.ds(0, (ncol - 1) * tb)], agc_r)

    two = 2 * tb

    def stage_a(s):
        j = lax.rem(d + s, nd)
        part = jnp.dot(everyone[0], wp[j], preferred_element_type=F32)
        xsend[s] = part.astype(BF16)
        for i in range(1, nx):
            other = lax.rem(x + i, nx)
            send(xsend.at[s, pl.ds(other * two, two)], xrecv.at[s, i - 1], x_s, x_r.at[s], xdev(i))

    def stage_y(s):
        mine = everyone.at[s, pl.ds(col * tb, tb)]
        wait_bytes(mine, agz_r.at[s])
        for i in range(1, ncol):
            send(mine, mine, agy_s, agy_r.at[s], cdev(i))

    def stage_b(s):
        wait_bytes(xrecv.at[s], x_r.at[s])

        def total(half):
            out = xsend[s, pl.ds(x * two + half * tb, tb)].astype(F32)
            for i in range(nx - 1):
                out = out + xrecv[s, i, pl.ds(half * tb, tb)].astype(F32)
            return out

        zsend[s] = total(1 - h).astype(BF16)
        send(zsend.at[s], zrecv.at[s], z_s, z_r.at[s], zdev(lax.rem(z + nd, nz)))
        zown[s] = total(h)

    def stage_c(s):
        j = lax.rem(d + s, nd)
        wait_bytes(zrecv.at[s], z_r.at[s])
        both = zown[s] + zrecv[s].astype(F32)
        gate, upper = both[:, :pad], both[:, pad:]
        sig = jax.nn.sigmoid(gate)
        act = gate * sig
        slope = cotp[j].astype(F32)
        hidp[j] = (act * upper).astype(BF16)
        dsend[s, :, :pad] = (slope * upper * sig * (1.0 + gate * (1.0 - sig))).astype(BF16)
        dsend[s, :, pad:] = (slope * act).astype(BF16)
        there = dall.at[s, pl.ds(row * tb, tb)]

        @pl.when(s == 0)
        def _():
            dall[0, pl.ds(row * tb, tb)] = dsend[0]
            send(dsend.at[0], there, dz_s, dz_r.at[s], (x * 2 + 1 - h, col, d))

        @pl.when(s > 0)
        def _():
            send(dsend.at[s], there, dz_s, dz_r.at[s], (x * 2, col, j))
            send(dsend.at[s], there, dz_s, dz_r.at[s], (x * 2 + 1, col, j))

    def stage_d(s):
        @pl.when(s == 0)
        def _():
            wait_bytes(dall.at[0, pl.ds(0, tb)], dz_r.at[0])

        @pl.when(s > 0)
        def _():
            wait_bytes(dall.at[s, pl.ds(0, two)], dz_r.at[s])

        mine = dall.at[s, pl.ds(x * two, two)]
        for i in range(1, nx):
            send(mine, mine, dx_s, dx_r.at[s], xdev(i))

    def stage_e(s):
        wait_bytes(dall.at[s, pl.ds(0, (nx - 1) * two)], dx_r.at[s])
        part = lax.dot_general(dall[s], wp[d], (((1,), (1,)), ((), ())), preferred_element_type=F32)
        gsend[s] = part.astype(BF16)
        for i in range(1, ncol):
            other = lax.rem(col + i, ncol)
            send(gsend.at[s, pl.ds(other * tb, tb)], grecv.at[s, i - 1], g_s, g_r.at[s], cdev(i))

        @pl.when(s > 0)
        def _():
            wait_bytes(everyone.at[s, pl.ds(0, (ncol - 1) * tb)], agy_r.at[s])

        acc[...] += lax.dot_general(everyone[s], dall[s], (((0,), (0,)), ((), ())), preferred_element_type=F32)

    def stage_f(s):
        wait_bytes(grecv.at[s], g_r.at[s])
        out = gsend[s, pl.ds(col * tb, tb)].astype(F32)
        for i in range(ncol - 1):
            out = out + grecv[s, i].astype(F32)

        @pl.when(s == 0)
        def _():
            giown[...] = out

        @pl.when(s > 0)
        def _():
            fsend[s] = out.astype(BF16)
            send(fsend.at[s], frecv.at[s], f_s, f_r.at[s], (row, col, lax.rem(d - s + nd, nd)))

    stages = ((stage_a, 0, 0), (stage_b, 1, 0), (stage_y, 0, 1), (stage_c, 3, 0), (stage_d, 5, 0), (stage_e, 6, 0), (stage_f, 7, 0))
    steps = nd + 7

    def body(t, carry):
        for fn, lag, first in stages:
            s = t - lag

            @pl.when((s >= first) & (s < nd))
            def _(fn=fn, s=s):
                fn(s)

        return carry

    lax.fori_loop(0, steps, body, None)

    for j in range(nd):
        hid_ref[0, :, j * sub : (j + 1) * sub] = hidp[j, :, :sub]
    gg_ref[...] = acc[:, :sub].astype(BF16)
    gu_ref[...] = acc[:, pad : pad + sub].astype(BF16)
    out = giown[...]
    for s in range(1, nd):
        wait_bytes(frecv.at[s], f_r.at[s])
        out = out + frecv[s].astype(F32)
    gi_ref[0] = out.astype(BF16)

    wait_bytes(everyone.at[0, pl.ds(0, (ncol - 1) * tb)], agc_s)
    wait_bytes(everyone.at[0, pl.ds(0, (nd - 1) * tb)], agz_s)
    wait_bytes(everyone.at[pl.ds(0, nd - 1), pl.ds(0, (ncol - 1) * tb)], agy_s)
    wait_bytes(xsend.at[:, pl.ds(0, (nx - 1) * two)], x_s)
    wait_bytes(zsend, z_s)
    wait_bytes(dsend, dz_s)
    wait_bytes(dsend.at[pl.ds(0, nd - 1)], dz_s)
    wait_bytes(dall.at[:, pl.ds(0, (nx - 1) * two)], dx_s)
    wait_bytes(gsend.at[:, pl.ds(0, (ncol - 1) * tb)], g_s)
    wait_bytes(fsend.at[pl.ds(0, nd - 1)], f_s)


def local(nx, ncol, nd, inputs, w_gate, w_up, cotangent):
    tb, feat = inputs.shape[1], inputs.shape[2]
    ff = w_gate.shape[1]
    sub = ff // nd
    pad = -(-sub // 128) * 128
    wide = 2 * pad
    tok = tb * ncol
    dma = pltpu.SemaphoreType.DMA
    any_spec = pl.BlockSpec(memory_space=pl.ANY)
    vmem = pl.BlockSpec(memory_space=pltpu.VMEM)
    return pl.pallas_call(
        functools.partial(kernel, nx, ncol, nd, sub, pad, tb),
        name="swiglu",
        out_shape=(
            jax.ShapeDtypeStruct((1, tb, ff), BF16),
            jax.ShapeDtypeStruct((1, tb, feat), BF16),
            jax.ShapeDtypeStruct((feat, sub), BF16),
            jax.ShapeDtypeStruct((feat, sub), BF16),
        ),
        in_specs=[any_spec] * 4,
        out_specs=(vmem,) * 4,
        scratch_shapes=[
            pltpu.VMEM((feat, ff), BF16),
            pltpu.VMEM((feat, ff), BF16),
            pltpu.VMEM((tb, ff), BF16),
            pltpu.VMEM((nd, feat, wide), BF16),
            pltpu.VMEM((nd, tb, pad), BF16),
            pltpu.VMEM((nd, tb, pad), BF16),
            pltpu.VMEM((nd, tok, feat), BF16),
            pltpu.VMEM((nd, tok, wide), BF16),
            pltpu.VMEM((nd, nx - 1, 2 * tb, wide), BF16),
            pltpu.VMEM((nd, tb, wide), F32),
            pltpu.VMEM((nd, tb, wide), BF16),
            pltpu.VMEM((nd, tb, wide), BF16),
            pltpu.VMEM((nd, tb, wide), BF16),
            pltpu.VMEM((nd, tok, wide), BF16),
            pltpu.VMEM((nd, tok, feat), BF16),
            pltpu.VMEM((nd, ncol - 1, tb, feat), BF16),
            pltpu.VMEM((nd, tb, feat), BF16),
            pltpu.VMEM((nd, tb, feat), BF16),
            pltpu.VMEM((feat, wide), F32),
            pltpu.VMEM((tb, feat), F32),
            dma((4,)),
            dma, dma,
            dma, dma((nd,)),
            dma, dma((nd,)),
            dma, dma((nd,)),
            dma, dma((nd,)),
            dma, dma((nd,)),
            dma, dma((nd,)),
            dma, dma((nd,)),
            dma, dma((nd,)),
        ],
        compiler_params=pltpu.CompilerParams(
            collective_id=0, has_side_effects=True, vmem_limit_bytes=50 * 2**20
        ),
    )(inputs, w_gate, w_up, cotangent)


def solution(mesh):
    nx, ncol, nd = mesh.shape["row"] // 2, mesh.shape["col"], mesh.shape["dp"]
    in_specs = (P("dp", "col", "row"), P("row", "col"), P("row", "col"), P("dp", "row", "col"))
    out_specs = (
        P("dp", "row", "col"),
        P("dp", "col", "row"),
        P("row", ("col", "dp")),
        P("row", ("col", "dp")),
    )
    return jax.shard_map(
        functools.partial(local, nx, ncol, nd), mesh=mesh, in_specs=in_specs, out_specs=out_specs, check_vma=False
    )
```

time: 510 us -> 110 us (0.22)
  waiting for transfers between devices: 197 us -> 0 us
  blocking collectives: 177 us -> 0 us
  Pallas kernels: 0 us -> 103 us
  starting transfers between devices: 94.4 us -> 0 us
  between operations: 15.6 us -> 0.65 us
  matrix products: 12.5 us -> 0 us
  other arithmetic: 8.12 us -> 0 us
    all_gather x3 -> x0, blocking collectives: 177 us -> none  [the longest x1 85.7 us: local(): lax.all_gather(d_gate, 'row', axis=0, tiled=True)]
    reduce_scatter x2 -> x0, waiting for transfers between devices: 170 us -> none  [the longest x1 137 us: local(): lax.psum_scatter(jnp.concatenate([first, second], axis=1).astype(jnp.bflo...]
    pallas_call x0 -> x1, Pallas kernels: none -> 103 us  [local(): pl.pallas_call(functools.partial(kernel, nx, ncol, nd, sub, pad, tb), nam...]
    all_to_all x2 -> x0, starting transfers between devices: 94.3 us -> none  [the longest x1 89.9 us: local(): lax.all_to_all(full_up, 'dp', split_axis=1, concat_axis=0, tiled=True)]
    all_to_all x2 -> x0, waiting for transfers between devices: 27.1 us -> none  [the longest x1 20.6 us: local(): lax.all_to_all(full_up, 'dp', split_axis=1, concat_axis=0, tiled=True)]
    dot_general x6 -> x0, matrix products: 12.5 us -> none  [the longest x1 3.78 us: replica_sum(): lax.dot_general(everyone, stacked_up, bdims, preferred_element_type=jnp.f...]
  transfers between devices with their start and end apart: 5 -> 0, of which waited for: 4 -> 0; matrix products, arithmetic and copies ran while one was open for 3% -> 0% of each run, Pallas kernels for 0% -> 0%
where the time goes in v1:
time: 110 us
  Pallas kernels  103 us (94%)
  local copies, waits for them, and re-layouts  6.05 us (6%)
    pallas_call x1, Pallas kernels, local(): pl.pallas_call(functools.partial(kernel, nx, ncol, nd, sub, pad, tb), nam...  103 us
    unnamed x8, local copies, waits for them, and re-layouts  4.41 us

profile of v1, /device:TPU:1, one launch (start us, length us, event | category | flops | bytes accessed | tf_op | source)
XLA Modules:
  0.0 109.6 jit_solution(1954776773540651031)
XLA Ops:
  0.6 0.0 copy-start
  0.6 1.5 %copy-done = bf16[512,1792]{1,0:T(8,128)(2,1)S(1)} copy-done((bf16[512,1792]{1,0:T(8,128)(2,1)S(1)}, bf16[512,1792]{1,0:T(8,128)(2,1)}, u32[]{:S(2)}) %copy-start) | copy-done | bytes 1835032
  2.1 0.0 copy-start.1
  2.1 0.9 copy-done.1
  3.0 0.0 copy-start.2
  3.0 0.8 copy-done.2
  3.8 102.9 %swiglu.1 = (bf16[1,32,1792]{2,1,0:T(8,128)(2,1)S(1)}, bf16[1,32,512]{2,1,0:T(8,128)(2,1)S(1)}, bf16[512,224]{1,0:T(8,128)(2,1)S(1)}, bf16[512,224]{1,0:T(8,128)(2,1)S(1)}) custom-call(bf16[1,32,512]{2,1,0:T(8,128)(2,1)S(1)} %copy-done.2, bf16[512,1792]{1,0:T(8,128)(2,1)S(1)} %copy-done, bf16[512,1792]{1,0:T(8,128)(2,1)} %wu_ref.1, ...), custom_call_target="tpu_custom_call" | custom-call | tf_op jit(solution)/shard_map/swiglu/pallas_call | solution.py:226
  106.7 0.8 copy.8
  107.6 0.8 copy.9
  108.4 0.6 copy.12
  109.0 0.6 copy.13
Async XLA Ops:
  0.6 1.5 %copy-start = (bf16[512,1792]{1,0:T(8,128)(2,1)S(1)}, bf16[512,1792]{1,0:T(8,128)(2,1)}, u32[]{:S(2)}) copy-start(bf16[512,1792]{1,0:T(8,128)(2,1)} %wg_ref.1) | copy-start | bytes 5505028
  2.1 0.9 copy-start.1
  3.0 0.8 copy-start.2

commit v2 on v1

v2 whole, which is shorter than its diff:
```python
import functools

import jax
import jax.numpy as jnp
from jax import lax
from jax.experimental import pallas as pl
from jax.experimental.pallas import tpu as pltpu
from jax.sharding import PartitionSpec as P

MESH = pl.DeviceIdType.MESH
F32 = jnp.float32
BF16 = jnp.bfloat16
LANES = 128
PIECES = ((0, 128), (128, 192), (192, 224))
DLAG = 8
VMEM_LIMIT = 53 * 2**20


def wait_bytes(ref, sem):
    pltpu.make_async_copy(ref, ref, sem).wait()


def kernel(
    nx, ny, nd, sub, tb,
    in_ref, wg_ref, wu_ref, cot_ref,
    hid_ref, gi_ref, gg_ref, gu_ref,
    wg, wu, cot, wp, cotp, hidp, everyone, xsend, xrecv, zown, zsend, zrecv, dsend, dall, dfull,
    gsend, gsib, gy, grecv, fsend, frecv, acc, giown,
    hello, loc, agc_s, agc_r, agz_s, agz_r, agy_s, agy_r, agk_s, agk_r, x_s, x_r, z_s, z_r, dz_s, dz_r, dx_s, dx_r,
    gk_s, gk_r, g_s, g_r, f_s, f_r,
):
    row, col, d = lax.axis_index("row"), lax.axis_index("col"), lax.axis_index("dp")
    x, h = row // 2, row % 2
    y, k = col // 2, col % 2
    nz, ncol = 2 * nd, 2 * ny
    z = h * nd + d
    feat = wg.shape[0]
    seven = frecv
    sibling = (row, y * 2 + 1 - k, d)

    def zdev(z2):
        return (x * 2 + z2 // nd, col, z2 % nd)

    def xdev(i):
        return (lax.rem(x + i, nx) * 2 + h, col, d)

    def ydev(i):
        return (row, lax.rem(y + i, ny) * 2 + k, d)

    def cdev(i):
        return (row, lax.rem(col + i, ncol), d)

    def rank(z2):
        return jnp.minimum(z2, nd)

    def send(src, dst, ssem, rsem, dev):
        pltpu.make_async_remote_copy(
            src_ref=src, dst_ref=dst, send_sem=ssem, recv_sem=rsem, device_id=dev, device_id_type=MESH
        ).start()

    barrier = pltpu.get_barrier_semaphore()
    for i in range(1, ncol):
        pl.semaphore_signal(barrier, inc=1, device_id=cdev(i), device_id_type=MESH)
    for i in range(1, nx):
        pl.semaphore_signal(barrier, inc=1, device_id=xdev(i), device_id_type=MESH)
    my_rank = rank(z)
    for i in range(1, nz):
        z2 = lax.rem(z + i, nz)

        @pl.when((rank(z2) > my_rank) | ((h == 1) & (z2 >= nd)))
        def _(z2=z2):
            pl.semaphore_signal(barrier, inc=1, device_id=zdev(z2), device_id_type=MESH)

    loads = [
        pltpu.make_async_copy(wg_ref, wg, loc.at[0]),
        pltpu.make_async_copy(wu_ref, wu, loc.at[1]),
        pltpu.make_async_copy(cot_ref.at[0], cot, loc.at[2]),
        pltpu.make_async_copy(in_ref.at[0], everyone.at[0, y, k], loc.at[3]),
    ]
    for load in loads:
        load.start()
    pl.semaphore_wait(barrier, ncol - 1 + nx - 1 + jnp.where(h == 0, d, nz - 1))

    for i in range(1, ncol):
        send(in_ref.at[0], everyone.at[0, y, k], agc_s, agc_r, cdev(i))
    for i in range(1, nz):
        z2 = lax.rem(z + i, nz)

        @pl.when(rank(z2) < my_rank)
        def _(z2=z2):
            pl.semaphore_signal(hello.at[h], inc=1, device_id=zdev(z2), device_id_type=MESH)

    def gather_z():
        for i in range(1, nd):
            send(in_ref.at[0], everyone.at[i, y, k], agz_s, agz_r.at[i], (row, col, lax.rem(d + i, nd)))

    @pl.when(h == 1)
    def _():
        gather_z()

    for load in loads:
        load.wait()

    @pl.loop(0, feat // 64)
    def _(q):
        rows = pl.ds(pl.multiple_of(q * 64, 64), 64)
        for j in range(nd):
            o = j * sub
            at = 0
            for lo, hi in PIECES:
                for w in (wg, wu):
                    wp[j, rows, at : at + hi - lo] = w[rows, o + lo : o + hi]
                    at += hi - lo
            wp[j, rows, at:] = jnp.zeros((64, 4 * LANES - at), BF16)

    cotp[...] = jnp.zeros_like(cotp)
    half = tb // 2
    for j in range(nd):
        o = j * sub
        cotp[j, :tb, :] = cot[:, o : o + 128]
        cotp[j, tb : 2 * tb, :64] = cot[:, o + 128 : o + 192]
        cotp[j, 2 * tb :, :32] = cot[:half, o + 192 : o + 224]
        cotp[j, 2 * tb :, 64:96] = cot[half:, o + 192 : o + 224]
    acc[...] = jnp.zeros_like(acc)
    wait_bytes(seven.at[pl.ds(0, ncol - 1)], agc_r)

    def stage_a(s):
        j = lax.rem(d + s, nd)
        part = jnp.dot(everyone[0].reshape(ncol * tb, feat), wp[j], preferred_element_type=F32)
        for c in range(3):
            xsend[s, :, c * tb : (c + 1) * tb, :] = (
                part[:, c * LANES : (c + 1) * LANES].reshape(2 * nx, tb, LANES).astype(BF16)
            )
        last = part[:, 3 * LANES :].reshape(2 * nx, 2, half, LANES)
        low, high = last[:, 0].reshape(nx * tb, LANES), last[:, 1].reshape(nx * tb, LANES)
        xsend[s, :, 3 * tb :, :] = (low + pltpu.roll(high, 64, 1)).reshape(2 * nx, half, LANES).astype(BF16)
        for i in range(1, nx):
            other = lax.rem(x + i, nx)
            send(xsend.at[s, pl.ds(other * 2, 2)], xrecv.at[s, i - 1], x_s, x_r.at[s], xdev(i))

    def stage_agz(s):
        @pl.when((h == 0) & (d < nd - 1))
        def _():
            pl.semaphore_wait(hello.at[0], nd - 1 - d)

        @pl.when(h == 0)
        def _():
            gather_z()

    def stage_y(s):
        mine = everyone.at[s, y, k]
        wait_bytes(mine, agz_r.at[s])
        for i in range(1, ny):
            send(mine, mine, agy_s, agy_r.at[s], ydev(i))

    def stage_k(s):
        wait_bytes(everyone.at[s, pl.ds(0, ny - 1), k], agy_r.at[s])
        mine = everyone.at[s, :, k]
        send(mine, mine, agk_s, agk_r.at[s], sibling)

    def stage_b(s):
        wait_bytes(xrecv.at[s], x_r.at[s])

        def total(which):
            out = xsend[s, x * 2 + which].astype(F32)
            for i in range(nx - 1):
                out = out + xrecv[s, i, which].astype(F32)
            return out

        zsend[s] = total(1 - h).astype(BF16)

        @pl.when((s == nd - 1) & (h == 0))
        def _():
            pl.semaphore_wait(hello.at[1], nd)

        send(zsend.at[s], zrecv.at[s], z_s, z_r.at[s], zdev(lax.rem(z + nd, nz)))
        zown[s] = total(h)

    def stage_c(s):
        j = lax.rem(d + s, nd)
        wait_bytes(zrecv.at[s], z_r.at[s])
        both = zown[s] + zrecv[s].astype(F32)
        mid, end = both[2 * tb : 3 * tb], both[3 * tb :]
        gate = jnp.concatenate([both[:tb], mid, end], axis=0)
        upper = jnp.concatenate([both[tb : 2 * tb], pltpu.roll(mid, 64, 1), pltpu.roll(end, 96, 1)], axis=0)
        sig = jax.nn.sigmoid(gate)
        act = gate * sig
        slope = cotp[j].astype(F32)
        hidp[j] = (act * upper).astype(BF16)
        d_gate = slope * upper * sig * (1.0 + gate * (1.0 - sig))
        d_up = slope * act
        dsend[s, :tb, :] = d_gate[:tb].astype(BF16)
        dsend[s, tb : 2 * tb, :] = d_up[:tb].astype(BF16)
        dsend[s, 2 * tb : 3 * tb, :] = (d_gate[tb : 2 * tb] + pltpu.roll(d_up[tb : 2 * tb], 64, 1)).astype(BF16)
        dsend[s, 3 * tb :, :] = (d_gate[2 * tb :] + pltpu.roll(d_up[2 * tb :], 32, 1)).astype(BF16)
        there = dall.at[s, row]

        @pl.when(s == 0)
        def _():
            dall[0, row] = dsend[0]
            send(dsend.at[0], there, dz_s, dz_r.at[s], (x * 2 + 1 - h, col, d))

        @pl.when(s > 0)
        def _():
            send(dsend.at[s], there, dz_s, dz_r.at[s], (x * 2, col, j))
            send(dsend.at[s], there, dz_s, dz_r.at[s], (x * 2 + 1, col, j))

    def stage_d(s):
        @pl.when(s == 0)
        def _():
            wait_bytes(dall.at[0, 0], dz_r.at[0])

        @pl.when(s > 0)
        def _():
            wait_bytes(dall.at[s, pl.ds(0, 2)], dz_r.at[s])

        mine = dall.at[s, pl.ds(x * 2, 2)]
        for i in range(1, nx):
            send(mine, mine, dx_s, dx_r.at[s], xdev(i))

    def stage_e(s):
        wait_bytes(dall.at[s, pl.ds(0, (nx - 1) * 2)], dx_r.at[s])
        for c in range(3):
            dfull[:, c * LANES : (c + 1) * LANES] = dall[s, :, c * tb : (c + 1) * tb, :].reshape(2 * nx * tb, LANES)
        low = dall[s, :, 3 * tb :, :].astype(F32)
        high = pltpu.roll(low.reshape(nx * tb, LANES), 64, 1).reshape(2 * nx, half, LANES)
        dfull[:, 3 * LANES :] = jnp.concatenate([low, high], axis=1).reshape(2 * nx * tb, LANES).astype(BF16)
        part = lax.dot_general(dfull[...], wp[d], (((1,), (1,)), ((), ())), preferred_element_type=F32)
        gsend[s] = part.astype(BF16).reshape(ny, 2, tb, feat)
        send(gsend.at[s, :, 1 - k], gsib.at[s], gk_s, gk_r.at[s], sibling)

        @pl.when(s > 0)
        def _():
            wait_bytes(everyone.at[s, :, k], agk_r.at[s])

        acc[...] += lax.dot_general(
            dfull[...], everyone[s].reshape(ncol * tb, feat), (((0,), (0,)), ((), ())), preferred_element_type=F32
        )

    def stage_f(s):
        wait_bytes(gsib.at[s], gk_r.at[s])
        for i in range(1, ny):
            other = lax.rem(y + i, ny)
            gy[s, i - 1] = (gsend[s, other, k].astype(F32) + gsib[s, other].astype(F32)).astype(BF16)
            send(gy.at[s, i - 1], grecv.at[s, i - 1], g_s, g_r.at[s], ydev(i))

    def stage_h(s):
        wait_bytes(grecv.at[s], g_r.at[s])
        out = gsend[s, y, k].astype(F32) + gsib[s, y].astype(F32)
        for i in range(ny - 1):
            out = out + grecv[s, i].astype(F32)

        @pl.when(s == 0)
        def _():
            giown[...] = out

        @pl.when(s > 0)
        def _():
            fsend[s] = out.astype(BF16)
            send(fsend.at[s], frecv.at[s], f_s, f_r.at[s], (row, col, lax.rem(d - s + nd, nd)))

    def stage_hidden(s):
        for j in range(nd):
            o = j * sub
            hid_ref[0, :, o : o + 128] = hidp[j, :tb, :]
            hid_ref[0, :, o + 128 : o + 192] = hidp[j, tb : 2 * tb, :64]
            hid_ref[0, :half, o + 192 : o + 224] = hidp[j, 2 * tb :, :32]
            hid_ref[0, half:, o + 192 : o + 224] = hidp[j, 2 * tb :, 64:96]

    def stage_weights(s):
        at = 0
        for lo, hi in PIECES:
            for out_ref in (gg_ref, gu_ref):
                out_ref[lo:hi, :] = acc[at : at + hi - lo, :].astype(BF16)
                at += hi - lo

    last = nd - 1
    stages = (
        (stage_a, 0, 0, 2), (stage_a, -1, 3, last), (stage_agz, 1, 0, 0), (stage_b, 1, 0, last), (stage_c, 4, 0, last),
        (stage_y, 5, 0, last - 1), (stage_k, 7, 0, last - 1), (stage_d, DLAG, 0, last), (stage_e, DLAG + 2, 0, last),
        (stage_f, DLAG + 3, 0, last), (stage_h, DLAG + 4, 0, last), (stage_hidden, 13, 0, 0), (stage_weights, DLAG + 10, 0, 0),
    )

    def body(t, carry):
        for fn, lag, low, high in stages:

            @pl.when((t >= lag + low) & (t <= lag + high))
            def _(fn=fn, lag=lag):
                fn(last - (t - lag))

        return carry

    lax.fori_loop(0, nd + DLAG + 4, body, None)

    out = giown[...]
    for s in range(1, nd):
        wait_bytes(frecv.at[s], f_r.at[s])
        out = out + frecv[s].astype(F32)
    gi_ref[0] = out.astype(BF16)

    wait_bytes(seven.at[pl.ds(0, ncol - 1)], agc_s)
    wait_bytes(seven.at[pl.ds(0, nd - 1)], agz_s)
    wait_bytes(everyone.at[pl.ds(0, nd - 1), pl.ds(0, ny - 1), 0], agy_s)
    wait_bytes(everyone.at[pl.ds(0, nd - 1), :, 0], agk_s)
    wait_bytes(xsend.at[:, pl.ds(0, (nx - 1) * 2)], x_s)
    wait_bytes(zsend, z_s)
    wait_bytes(dsend, dz_s)
    wait_bytes(dsend.at[pl.ds(0, nd - 1)], dz_s)
    wait_bytes(dall.at[:, pl.ds(0, (nx - 1) * 2)], dx_s)
    wait_bytes(gsib, gk_s)
    wait_bytes(gy, g_s)
    wait_bytes(fsend.at[pl.ds(0, nd - 1)], f_s)


def local(nx, ny, nd, inputs, w_gate, w_up, cotangent):
    tb, feat = inputs.shape[1], inputs.shape[2]
    ff = w_gate.shape[1]
    sub = ff // nd
    wide = 4 * LANES
    tok = tb * 2 * ny
    rows = tb * 7 // 2
    dma = pltpu.SemaphoreType.DMA
    any_spec = pl.BlockSpec(memory_space=pl.ANY)
    vmem = pl.BlockSpec(memory_space=pltpu.VMEM)
    hidden, grad_inputs, grad_gate, grad_up = pl.pallas_call(
        functools.partial(kernel, nx, ny, nd, sub, tb),
        name="swiglu",
        out_shape=(
            jax.ShapeDtypeStruct((1, tb, ff), BF16),
            jax.ShapeDtypeStruct((1, tb, feat), BF16),
            jax.ShapeDtypeStruct((sub, feat), BF16),
            jax.ShapeDtypeStruct((sub, feat), BF16),
        ),
        in_specs=[any_spec] * 4,
        out_specs=(vmem,) * 4,
        scratch_shapes=[
            pltpu.VMEM((feat, ff), BF16),
            pltpu.VMEM((feat, ff), BF16),
            pltpu.VMEM((tb, ff), BF16),
            pltpu.VMEM((nd, feat, wide), BF16),
            pltpu.VMEM((nd, tb * 5 // 2, LANES), BF16),
            pltpu.VMEM((nd, tb * 5 // 2, LANES), BF16),
            pltpu.VMEM((nd, ny, 2, tb, feat), BF16),
            pltpu.VMEM((nd, 2 * nx, rows, LANES), BF16),
            pltpu.VMEM((nd, nx - 1, 2, rows, LANES), BF16),
            pltpu.VMEM((nd, rows, LANES), F32),
            pltpu.VMEM((nd, rows, LANES), BF16),
            pltpu.VMEM((nd, rows, LANES), BF16),
            pltpu.VMEM((nd, rows, LANES), BF16),
            pltpu.VMEM((nd, 2 * nx, rows, LANES), BF16),
            pltpu.VMEM((tok, wide), BF16),
            pltpu.VMEM((nd, ny, 2, tb, feat), BF16),
            pltpu.VMEM((nd, ny, tb, feat), BF16),
            pltpu.VMEM((nd, ny - 1, tb, feat), BF16),
            pltpu.VMEM((nd, ny - 1, tb, feat), BF16),
            pltpu.VMEM((nd, tb, feat), BF16),
            pltpu.VMEM((nd, tb, feat), BF16),
            pltpu.VMEM((wide, feat), F32),
            pltpu.VMEM((tb, feat), F32),
            pltpu.SemaphoreType.REGULAR((2,)),
            dma((4,)),
            dma, dma,
            dma, dma((nd,)),
            dma, dma((nd,)),
            dma, dma((nd,)),
            dma, dma((nd,)),
            dma, dma((nd,)),
            dma, dma((nd,)),
            dma, dma((nd,)),
            dma, dma((nd,)),
            dma, dma((nd,)),
            dma, dma((nd,)),
        ],
        compiler_params=pltpu.CompilerParams(
            collective_id=0, has_side_effects=True, vmem_limit_bytes=VMEM_LIMIT
        ),
    )(inputs, w_gate, w_up, cotangent)
    return hidden, grad_inputs, grad_gate.T, grad_up.T


def solution(mesh):
    nx, ny, nd = mesh.shape["row"] // 2, mesh.shape["col"] // 2, mesh.shape["dp"]
    in_specs = (P("dp", "col", "row"), P("row", "col"), P("row", "col"), P("dp", "row", "col"))
    out_specs = (
        P("dp", "row", "col"),
        P("dp", "col", "row"),
        P("row", ("col", "dp")),
        P("row", ("col", "dp")),
    )
    return jax.shard_map(
        functools.partial(local, nx, ny, nd), mesh=mesh, in_specs=in_specs, out_specs=out_specs, check_vma=False
    )
```

time: 110 us -> 98.1 us (0.89)
  Pallas kernels: 103 us -> 93 us
  local copies, waits for them, and re-layouts: 6.05 us -> 4.29 us
    pallas_call x1, Pallas kernels: 103 us -> 93 us  [local(): pl.pallas_call(functools.partial(kernel, nx, ny, nd, sub, tb), name='swig...]
    pallas_call x2 -> x0, local copies, waits for them, and re-layouts: 1.64 us -> none  [local(): pl.pallas_call(functools.partial(kernel, nx, ncol, nd, sub, pad, tb), nam...]
where the time goes in v2:
time: 98.1 us; the launch traced here: 97.9 us
  Pallas kernels  93 us (95%)
  local copies, waits for them, and re-layouts  4.29 us (4%)
    pallas_call x1, Pallas kernels, local(): pl.pallas_call(functools.partial(kernel, nx, ny, nd, sub, tb), name='swig...  93 us
    unnamed x8, local copies, waits for them, and re-layouts  4.29 us

profile of v2, /device:TPU:1, one launch (start us, length us, event | category | flops | bytes accessed | tf_op | source)
XLA Modules:
  0.0 97.9 jit_solution(7544124654494765088)
XLA Ops:
  0.6 0.0 copy-start
  0.6 0.9 copy-done
  1.5 0.0 copy-start.1
  1.5 0.8 copy-done.1
  2.3 93.0 %swiglu.1 = (bf16[1,32,1792]{2,1,0:T(8,128)(2,1)S(1)}, bf16[1,32,512]{2,1,0:T(8,128)(2,1)S(1)}, bf16[224,512]{1,0:T(8,128)(2,1)S(1)}, bf16[224,512]{1,0:T(8,128)(2,1)S(1)}) custom-call(bf16[1,32,512]{2,1,0:T(8,128)(2,1)S(1)} %copy-done.1, bf16[512,1792]{1,0:T(8,128)(2,1)} %wg_ref.1, bf16[512,1792]{1,0:T(8,128)(2,1)} %wu_ref.1, bf16[1,32,1792]{2,1,0:T(8,128)(2,1)S(1)} %copy-done), custom_call_target="tpu_custom_call" | custom-call | tf_op jit(solution)/shard_map/swiglu/pallas_call | solution.py:325
  95.3 0.6 copy.12
  95.9 0.6 copy.13
  96.5 0.7 copy.14
  97.2 0.7 copy.15
Async XLA Ops:
  0.6 0.9 copy-start
  1.5 0.8 copy-start.1

commit v3 on v2

--- a/solution.py
+++ b/solution.py
@@ -12,7 +12,9 @@
 BF16 = jnp.bfloat16
 LANES = 128
 PIECES = ((0, 128), (128, 192), (192, 224))
-DLAG = 8
+ALEAD, BLEAD, CLAG, C2, YLAG = 1, 0, 4, 0, 8
+LAGS = (7, 9, 10, 12)
+UPPER = 1
 VMEM_LIMIT = 53 * 2**20
 
 
@@ -90,13 +92,16 @@
         def _(z2=z2):
             pl.semaphore_signal(hello.at[h], inc=1, device_id=zdev(z2), device_id_type=MESH)
 
-    def gather_z():
+    def gather_z(when):
         for i in range(1, nd):
-            send(in_ref.at[0], everyone.at[i, y, k], agz_s, agz_r.at[i], (row, col, lax.rem(d + i, nd)))
-
-    @pl.when(h == 1)
-    def _():
-        gather_z()
+            d2 = lax.rem(d + i, nd)
+            near = (i == 1) & (d % 2 == 0) | (i == nd - 1) & (d % 2 == 1)
+
+            @pl.when(when(d2))
+            def _(i=i, d2=d2):
+                send(in_ref.at[0], everyone.at[i, y, k], agz_s, agz_r.at[i], (row, col, d2))
+
+    gather_z(lambda d2: (h == 1) | (d2 < d))
 
     for load in loads:
         load.wait()
@@ -142,14 +147,20 @@
         @pl.when((h == 0) & (d < nd - 1))
         def _():
             pl.semaphore_wait(hello.at[0], nd - 1 - d)
-
-        @pl.when(h == 0)
-        def _():
-            gather_z()
+            gather_z(lambda d2: d2 > d)
+
+    def stage_r(s):
+        for i in range(2, nd, 2):
+            here = everyone.at[i, y, k]
+            wait_bytes(here, agz_r.at[i])
+            there = i + 1 - 2 * (d % 2)
+            send(here, everyone.at[there, y, k], agz_s, agz_r.at[there], (row, col, d + 1 - 2 * (d % 2)))
 
     def stage_y(s):
         mine = everyone.at[s, y, k]
+
         wait_bytes(mine, agz_r.at[s])
+
         for i in range(1, ny):
             send(mine, mine, agy_s, agy_r.at[s], ydev(i))
 
@@ -198,12 +209,17 @@
         @pl.when(s == 0)
         def _():
             dall[0, row] = dsend[0]
-            send(dsend.at[0], there, dz_s, dz_r.at[s], (x * 2 + 1 - h, col, d))
-
-        @pl.when(s > 0)
-        def _():
-            send(dsend.at[s], there, dz_s, dz_r.at[s], (x * 2, col, j))
-            send(dsend.at[s], there, dz_s, dz_r.at[s], (x * 2 + 1, col, j))
+
+        send_d(s, 0)
+
+    def send_d(s, half_z):
+        @pl.when((s > 0) | (h != half_z))
+        def _():
+            there = dall.at[s, row]
+            send(dsend.at[s], there, dz_s, dz_r.at[s], (x * 2 + half_z, col, lax.rem(d + s, nd)))
+
+    def stage_c2(s):
+        send_d(s, 1)
 
     def stage_d(s):
         @pl.when(s == 0)
@@ -221,20 +237,21 @@
     def stage_e(s):
         wait_bytes(dall.at[s, pl.ds(0, (nx - 1) * 2)], dx_r.at[s])
         for c in range(3):
-            dfull[:, c * LANES : (c + 1) * LANES] = dall[s, :, c * tb : (c + 1) * tb, :].reshape(2 * nx * tb, LANES)
+            dfull[s, :, c * LANES : (c + 1) * LANES] = dall[s, :, c * tb : (c + 1) * tb, :].reshape(2 * nx * tb, LANES)
         low = dall[s, :, 3 * tb :, :].astype(F32)
         high = pltpu.roll(low.reshape(nx * tb, LANES), 64, 1).reshape(2 * nx, half, LANES)
-        dfull[:, 3 * LANES :] = jnp.concatenate([low, high], axis=1).reshape(2 * nx * tb, LANES).astype(BF16)
-        part = lax.dot_general(dfull[...], wp[d], (((1,), (1,)), ((), ())), preferred_element_type=F32)
+        dfull[s, :, 3 * LANES :] = jnp.concatenate([low, high], axis=1).reshape(2 * nx * tb, LANES).astype(BF16)
+        part = lax.dot_general(dfull[s], wp[d], (((1,), (1,)), ((), ())), preferred_element_type=F32)
         gsend[s] = part.astype(BF16).reshape(ny, 2, tb, feat)
         send(gsend.at[s, :, 1 - k], gsib.at[s], gk_s, gk_r.at[s], sibling)
 
+    def stage_w(s):
         @pl.when(s > 0)
         def _():
             wait_bytes(everyone.at[s, :, k], agk_r.at[s])
 
         acc[...] += lax.dot_general(
-            dfull[...], everyone[s].reshape(ncol * tb, feat), (((0,), (0,)), ((), ())), preferred_element_type=F32
+            dfull[s], everyone[s].reshape(ncol * tb, feat), (((0,), (0,)), ((), ())), preferred_element_type=F32
         )
 
     def stage_f(s):
@@ -275,10 +292,14 @@
                 at += hi - lo
 
     last = nd - 1
+    late = h * UPPER
+    lag_d, lag_e, lag_f, lag_h = (lag + late for lag in LAGS)
     stages = (
-        (stage_a, 0, 0, 2), (stage_a, -1, 3, last), (stage_agz, 1, 0, 0), (stage_b, 1, 0, last), (stage_c, 4, 0, last),
-        (stage_y, 5, 0, last - 1), (stage_k, 7, 0, last - 1), (stage_d, DLAG, 0, last), (stage_e, DLAG + 2, 0, last),
-        (stage_f, DLAG + 3, 0, last), (stage_h, DLAG + 4, 0, last), (stage_hidden, 13, 0, 0), (stage_weights, DLAG + 10, 0, 0),
+        (stage_a, 0, 0, 2), (stage_a, -ALEAD, 3, last), (stage_agz, 1, 0, 0), (stage_b, 1, 0, 2), (stage_b, 1 - BLEAD, 3, last),
+        (stage_c, CLAG, 0, last), (stage_c2, CLAG + C2, 0, last), (stage_y, YLAG, 0, last - 1),
+        (stage_k, YLAG + 2, 0, last - 1), (stage_d, lag_d, 0, last), (stage_e, lag_e, 0, last),
+        (stage_f, lag_f, 0, last), (stage_w, lag_h, 0, last), (stage_weights, lag_h, last, last), (stage_h, lag_h, 0, last),
+        (stage_hidden, 13, 0, 0),
     )
 
     def body(t, carry):
@@ -290,7 +311,7 @@
 
         return carry
 
-    lax.fori_loop(0, nd + DLAG + 4, body, None)
+    lax.fori_loop(0, nd + LAGS[3] + late, body, None)
 
     out = giown[...]
     for s in range(1, nd):
@@ -348,7 +369,7 @@
             pltpu.VMEM((nd, rows, LANES), BF16),
             pltpu.VMEM((nd, rows, LANES), BF16),
             pltpu.VMEM((nd, 2 * nx, rows, LANES), BF16),
-            pltpu.VMEM((tok, wide), BF16),
+            pltpu.VMEM((nd, tok, wide), BF16),
             pltpu.VMEM((nd, ny, 2, tb, feat), BF16),
             pltpu.VMEM((nd, ny, tb, feat), BF16),
             pltpu.VMEM((nd, ny - 1, tb, feat), BF16),

time: 98.1 us -> 94 us (0.958)
  Pallas kernels: 93 us -> 88.8 us
    pallas_call x1, Pallas kernels: 93 us -> 88.8 us  [local(): pl.pallas_call(functools.partial(kernel, nx, ny, nd, sub, tb), name='swig...]
where the time goes in v3:
time: 94 us; the launch traced here: 93.8 us
  Pallas kernels  88.8 us (94%)
  local copies, waits for them, and re-layouts  4.29 us (5%)
    pallas_call x1, Pallas kernels, local(): pl.pallas_call(functools.partial(kernel, nx, ny, nd, sub, tb), name='swig...  88.8 us
    unnamed x8, local copies, waits for them, and re-layouts  4.29 us

profile of v3, /device:TPU:1, one launch (start us, length us, event | category | flops | bytes accessed | tf_op | source)
XLA Modules:
  0.0 93.8 jit_solution(13637854018142544099)
XLA Ops:
  0.6 0.0 copy-start
  0.6 0.9 copy-done
  1.5 0.0 copy-start.1
  1.5 0.8 copy-done.1
  2.3 88.8 %swiglu.1 = (bf16[1,32,1792]{2,1,0:T(8,128)(2,1)S(1)}, bf16[1,32,512]{2,1,0:T(8,128)(2,1)S(1)}, bf16[224,512]{1,0:T(8,128)(2,1)S(1)}, bf16[224,512]{1,0:T(8,128)(2,1)S(1)}) custom-call(bf16[1,32,512]{2,1,0:T(8,128)(2,1)S(1)} %copy-done.1, bf16[512,1792]{1,0:T(8,128)(2,1)} %wg_ref.1, bf16[512,1792]{1,0:T(8,128)(2,1)} %wu_ref.1, bf16[1,32,1792]{2,1,0:T(8,128)(2,1)S(1)} %copy-done), custom_call_target="tpu_custom_call" | custom-call | tf_op jit(solution)/shard_map/swiglu/pallas_call | solution.py:346
  91.1 0.6 copy.12
  91.8 0.6 copy.13
  92.4 0.7 copy.14
  93.1 0.7 copy.15
Async XLA Ops:
  0.6 0.9 copy-start
  1.5 0.8 copy-start.1

commit v4 on v3

--- a/solution.py
+++ b/solution.py
@@ -24,8 +24,8 @@
 
 def kernel(
     nx, ny, nd, sub, tb,
-    in_ref, wg_ref, wu_ref, cot_ref,
-    hid_ref, gi_ref, gg_ref, gu_ref,
+    both_ref, wg_ref, wu_ref,
+    hid_ref, all_ref,
     wg, wu, cot, wp, cotp, hidp, everyone, xsend, xrecv, zown, zsend, zrecv, dsend, dall, dfull,
     gsend, gsib, gy, grecv, fsend, frecv, acc, giown,
     hello, loc, agc_s, agc_r, agz_s, agz_r, agy_s, agy_r, agk_s, agk_r, x_s, x_r, z_s, z_r, dz_s, dz_r, dx_s, dx_r,
@@ -37,6 +37,9 @@
     nz, ncol = 2 * nd, 2 * ny
     z = h * nd + d
     feat = wg.shape[0]
+    gg_ref, gu_ref = all_ref.at[pl.ds(0, sub)], all_ref.at[pl.ds(sub, sub)]
+    ff = wg.shape[1]
+    own = both_ref.at[:, pl.ds(ff, feat)]
     seven = frecv
     sibling = (row, y * 2 + 1 - k, d)
 
@@ -76,15 +79,15 @@
     loads = [
         pltpu.make_async_copy(wg_ref, wg, loc.at[0]),
         pltpu.make_async_copy(wu_ref, wu, loc.at[1]),
-        pltpu.make_async_copy(cot_ref.at[0], cot, loc.at[2]),
-        pltpu.make_async_copy(in_ref.at[0], everyone.at[0, y, k], loc.at[3]),
+        pltpu.make_async_copy(both_ref.at[:, pl.ds(0, ff)], cot, loc.at[2]),
+        pltpu.make_async_copy(own, everyone.at[0, y, k], loc.at[3]),
     ]
     for load in loads:
         load.start()
     pl.semaphore_wait(barrier, ncol - 1 + nx - 1 + jnp.where(h == 0, d, nz - 1))
 
     for i in range(1, ncol):
-        send(in_ref.at[0], everyone.at[0, y, k], agc_s, agc_r, cdev(i))
+        send(own, everyone.at[0, y, k], agc_s, agc_r, cdev(i))
     for i in range(1, nz):
         z2 = lax.rem(z + i, nz)
 
@@ -99,7 +102,7 @@
 
             @pl.when(when(d2))
             def _(i=i, d2=d2):
-                send(in_ref.at[0], everyone.at[i, y, k], agz_s, agz_r.at[i], (row, col, d2))
+                send(own, everyone.at[i, y, k], agz_s, agz_r.at[i], (row, col, d2))
 
     gather_z(lambda d2: (h == 1) | (d2 < d))
 
@@ -296,8 +299,8 @@
     lag_d, lag_e, lag_f, lag_h = (lag + late for lag in LAGS)
     stages = (
         (stage_a, 0, 0, 2), (stage_a, -ALEAD, 3, last), (stage_agz, 1, 0, 0), (stage_b, 1, 0, 2), (stage_b, 1 - BLEAD, 3, last),
-        (stage_c, CLAG, 0, last), (stage_c2, CLAG + C2, 0, last), (stage_y, YLAG, 0, last - 1),
-        (stage_k, YLAG + 2, 0, last - 1), (stage_d, lag_d, 0, last), (stage_e, lag_e, 0, last),
+        (stage_y, YLAG, 0, last - 1),
+        (stage_k, YLAG + 2, 0, last - 1), (stage_d, lag_d, 0, last), (stage_c, CLAG, 0, last), (stage_c2, CLAG + C2, 0, last), (stage_e, lag_e, 0, last),
         (stage_f, lag_f, 0, last), (stage_w, lag_h, 0, last), (stage_weights, lag_h, last, last), (stage_h, lag_h, 0, last),
         (stage_hidden, 13, 0, 0),
     )
@@ -317,7 +320,7 @@
     for s in range(1, nd):
         wait_bytes(frecv.at[s], f_r.at[s])
         out = out + frecv[s].astype(F32)
-    gi_ref[0] = out.astype(BF16)
+    all_ref[2 * sub :] = out.astype(BF16)
 
     wait_bytes(seven.at[pl.ds(0, ncol - 1)], agc_s)
     wait_bytes(seven.at[pl.ds(0, nd - 1)], agz_s)
@@ -343,17 +346,15 @@
     dma = pltpu.SemaphoreType.DMA
     any_spec = pl.BlockSpec(memory_space=pl.ANY)
     vmem = pl.BlockSpec(memory_space=pltpu.VMEM)
-    hidden, grad_inputs, grad_gate, grad_up = pl.pallas_call(
+    hidden, others = pl.pallas_call(
         functools.partial(kernel, nx, ny, nd, sub, tb),
         name="swiglu",
         out_shape=(
             jax.ShapeDtypeStruct((1, tb, ff), BF16),
-            jax.ShapeDtypeStruct((1, tb, feat), BF16),
-            jax.ShapeDtypeStruct((sub, feat), BF16),
-            jax.ShapeDtypeStruct((sub, feat), BF16),
+            jax.ShapeDtypeStruct((2 * sub + tb, feat), BF16),
         ),
-        in_specs=[any_spec] * 4,
-        out_specs=(vmem,) * 4,
+        in_specs=[any_spec] * 3,
+        out_specs=(vmem,) * 2,
         scratch_shapes=[
             pltpu.VMEM((feat, ff), BF16),
             pltpu.VMEM((feat, ff), BF16),
@@ -395,8 +396,8 @@
         compiler_params=pltpu.CompilerParams(
             collective_id=0, has_side_effects=True, vmem_limit_bytes=VMEM_LIMIT
         ),
-    )(inputs, w_gate, w_up, cotangent)
-    return hidden, grad_inputs, grad_gate.T, grad_up.T
+    )(jnp.concatenate([cotangent[0], inputs[0]], axis=1), w_gate, w_up)
+    return hidden, others[None, 2 * sub :], others[:sub].T, others[sub : 2 * sub].T
 
 
 def solution(mesh):

time: 94 us -> 91.8 us (0.977)
  local copies, waits for them, and re-layouts: 4.29 us -> 2.06 us
    unnamed x8 -> x1, local copies, waits for them, and re-layouts: 4.29 us -> 0.65 us
where the time goes in v4:
time: 91.8 us; the launch traced here: 91.7 us
  Pallas kernels  88 us (96%)
  local copies, waits for them, and re-layouts  2.06 us (2%)
  other arithmetic  0.93 us (1%)
    pallas_call x1, Pallas kernels, local(): pl.pallas_call(functools.partial(kernel, nx, ny, nd, sub, tb), name='swig...  88 us

profile of v4, /device:TPU:1, one launch (start us, length us, event | category | flops | bytes accessed | tf_op | source)
XLA Modules:
  0.0 91.7 jit_solution(1436680600826901867)
XLA Ops:
  0.6 0.9 %pad_maximum_fusion.both_ref = bf16[32,2304]{1,0:T(8,128)(2,1)S(1)} fusion(bf16[32,512]{1,0:T(8,128)(2,1)} %bitcast.9, bf16[32,1792]{1,0:T(8,128)(2,1)} %bitcast.8), kind=kLoop, calls=%fused_computation.2 | loop fusion | flops 294912 | bytes 294912 | tf_op jit(solution)/shard_map/concatenate | solution.py:399
  1.6 88.0 %swiglu.1 = (bf16[1,32,1792]{2,1,0:T(8,128)(2,1)S(1)}, bf16[480,512]{1,0:T(8,128)(2,1)S(1)}) custom-call(bf16[32,2304]{1,0:T(8,128)(2,1)S(1)} %pad_maximum_fusion.both_ref, bf16[512,1792]{1,0:T(8,128)(2,1)} %wg_ref.1, bf16[512,1792]{1,0:T(8,128)(2,1)} %wu_ref.1), custom_call_target="tpu_custom_call" | custom-call | tf_op jit(solution)/shard_map/swiglu/pallas_call | solution.py:349
  89.6 0.6 slice_bitcast_fusion.2
  90.2 0.8 slice_bitcast_fusion
  91.0 0.6 copy.9

commit v5 on v4

--- a/solution.py
+++ b/solution.py
@@ -86,7 +86,7 @@
         load.start()
     pl.semaphore_wait(barrier, ncol - 1 + nx - 1 + jnp.where(h == 0, d, nz - 1))
 
-    for i in range(1, ncol):
+    for i in sorted(range(1, ncol), key=lambda i: abs(i - ncol // 2)):
         send(own, everyone.at[0, y, k], agc_s, agc_r, cdev(i))
     for i in range(1, nz):
         z2 = lax.rem(z + i, nz)

time: 91.8 us -> 91.8 us (level)
  no operation moved by 1% of the time
where the time goes in v5:
time: 91.8 us; the launch traced here: 91.2 us
  Pallas kernels  87.6 us (95%)
  local copies, waits for them, and re-layouts  2.06 us (2%)
  other arithmetic  0.93 us (1%)
    pallas_call x1, Pallas kernels, local(): pl.pallas_call(functools.partial(kernel, nx, ny, nd, sub, tb), name='swig...  87.6 us

profile of v5, /device:TPU:1, one launch (start us, length us, event | category | flops | bytes accessed | tf_op | source)
XLA Modules:
  0.0 91.2 jit_solution(4737186527330927834)
XLA Ops:
  0.6 0.9 %pad_maximum_fusion.both_ref = bf16[32,2304]{1,0:T(8,128)(2,1)S(1)} fusion(bf16[32,512]{1,0:T(8,128)(2,1)} %bitcast.9, bf16[32,1792]{1,0:T(8,128)(2,1)} %bitcast.8), kind=kLoop, calls=%fused_computation.2 | loop fusion | flops 294912 | bytes 294912 | tf_op jit(solution)/shard_map/concatenate | solution.py:399
  1.6 87.6 %swiglu.1 = (bf16[1,32,1792]{2,1,0:T(8,128)(2,1)S(1)}, bf16[480,512]{1,0:T(8,128)(2,1)S(1)}) custom-call(bf16[32,2304]{1,0:T(8,128)(2,1)S(1)} %pad_maximum_fusion.both_ref, bf16[512,1792]{1,0:T(8,128)(2,1)} %wg_ref.1, bf16[512,1792]{1,0:T(8,128)(2,1)} %wu_ref.1), custom_call_target="tpu_custom_call" | custom-call | tf_op jit(solution)/shard_map/swiglu/pallas_call | solution.py:349
  89.2 0.6 slice_bitcast_fusion.2
  89.8 0.8 slice_bitcast_fusion
  90.6 0.6 copy.9
